TPU v7x, 128 devices: a whole 4x4x4 slice. The times are simulated.
128 devices in a mesh: row: 16 (over x, y_lo, core), col: 8 (over y_hi, z).
Axes of the slice: x: 4, y: 4 (y_hi: 2, y_lo: 2; y = y_hi * 2 + y_lo), z: 4, core: 2. Of those that a mesh axis runs over, the one named last changes fastest.
Arguments:
- a_values: bfloat16 [8192, 8192], P('row', 'col'), may hold values from -0.15625 to 0.15625
- b_values: bfloat16 [8192, 8192], P('row', 'col'), may hold values from -6 to 6
- a_pattern: int32 [64, 64], P('row', 'col'), may hold values from 0 to 1, as said below
- b_pattern: int32 [64, 64], P('row', 'col'), may hold values from 0 to 1, as said below
- c_pattern: int32 [64, 64], P('row', 'col'), may hold values from 0 to 1, as said below
- owner_list: int32 [64], replicated, may hold values from 0 to 63, as said below
Outputs:
- product: bfloat16 [8192, 8192], P('row', 'col')
Inputs may be any that keep to these rules, and one draw needn't show every extreme that they name: a_pattern is 0 or 1 for each block. b_pattern is 0 or 1 for each block. c_pattern is 0 or 1 for each block. owner_list is a permutation of 0 to 63 of the form owner_list[d * 4 + s] = ((d + shift_s) mod 16) * 4 + q_s, with q a permutation of the 4 slots, slots 2p and 2p+1 sharing one shift, the shifts of different pairs distinct and none zero.
All inputs are finite; a program needn't handle non-finite values.
Results may differ from a plain program's by a relative error of at most 0.001.
Values may be sent and summed in bfloat16 or wider, within the bound.
No kernel may reach another device: no remote copies, remote signals or barrier semaphores. Data moves between devices by JAX's collectives and lax.ppermute only.
A program may use at most 128 MiB of HBM per device.

v0:
```python
import jax
import jax.numpy as jnp
from jax import lax
from jax.sharding import PartitionSpec as P


def from_behind(value, axis, by):
    count = lax.axis_size(axis)
    return lax.ppermute(value, axis, [(i, (i + by) % count) for i in range(count)])


def expand(pattern, width):
    return jnp.repeat(jnp.repeat(pattern, width, axis=0), width, axis=1)


def local(a_values, b_values, a_pattern, b_pattern, c_pattern, owner_list):
    width = a_values.shape[0] // a_pattern.shape[0]
    masked_a = jnp.where(expand(a_pattern, width) > 0, a_values, jnp.zeros_like(a_values))
    masked_b = jnp.where(expand(b_pattern, width) > 0, b_values, jnp.zeros_like(b_values))
    local_cols = b_values.shape[1]
    b_panel = lax.all_gather(masked_b, "row", axis=0, tiled=True)
    full = jnp.dot(
        lax.all_gather(masked_a, "col", axis=1, tiled=True),
        b_panel,
        preferred_element_type=jnp.float32,
    )
    full = jnp.where(expand(c_pattern, width) > 0, full, jnp.float32(0.0))
    rounded = full.astype(jnp.bfloat16)
    row_count = lax.axis_size("row")
    blocks_here = a_pattern.shape[0]
    slot_shift = owner_list[:blocks_here] // blocks_here % row_count
    slot_source = owner_list[:blocks_here] % blocks_here
    pieces = []
    for slot in range(blocks_here):
        pieces.append(lax.dynamic_slice_in_dim(rounded, slot_source[slot] * width, width, 0))
    moving = jnp.stack(pieces, axis=0).reshape(blocks_here // 2, 2 * width, local_cols)
    pair_shift = slot_shift.reshape(blocks_here // 2, 2)[:, 0]
    steps_needed = (row_count - 1).bit_length()
    for level in range(steps_needed):
        arrived = from_behind(moving, "row", row_count - (1 << level))
        taken = pair_shift // (1 << level) % 2 > 0
        moving = jnp.where(taken[:, None, None], arrived, moving)
    return moving.reshape(blocks_here * width, local_cols)


def solution(mesh):
    return jax.shard_map(
        local,
        mesh=mesh,
        in_specs=(
            P("row", "col"),
            P("row", "col"),
            P("row", "col"),
            P("row", "col"),
            P("row", "col"),
            P(),
        ),
        out_specs=P("row", "col"),
        check_vma=False,
    )
```

profile of v0, /device:TPU:1, one launch (start us, length us, event | category | flops | bytes accessed | tf_op | source)
XLA Modules:
  0.0 328.8 jit_solution(11265720749008335849)
XLA Ops:
  6.5 0.0 all-gather.3.cloned.1.call-start
  6.5 0.7 broadcast_compare_fusion.1
  7.3 1.6 broadcast_in_dim.56
  8.9 2.5 bitcast_select_fusion.1
  11.4 0.0 all-gather.3.cloned.1.call-update
  11.4 0.0 all-gather.5.cloned.1.call-start
  11.4 0.7 broadcast_compare_fusion
  12.2 1.6 broadcast_in_dim.58
  13.8 2.6 bitcast_select_fusion
  16.3 0.0 all-gather.5.cloned.1.call-update
  16.4 0.0 copy-done.1
  16.4 0.6 fusion.10
  19.7 102.0 %all-gather.3.cloned.1.call-done = bf16[512,8192]{1,0:T(8,128)(2,1)} async-done(((bf16[512,1024]{1,0:T(8,128)(2,1)}), bf16[512,8192]{1,0:T(8,128)(2,1)}) %all-gather.3.cloned.1.call-update) | async-done | bytes 8388624 | tf_op jit(solution)/shard_map/all_gather | solution.py:23
  121.6 91.9 %all-gather.5.cloned.1.call-done = bf16[8192,1024]{1,0:T(8,128)(2,1)} async-done(((bf16[512,1024]{1,0:T(8,128)(2,1)}), bf16[8192,1024]{1,0:T(8,128)(2,1)}) %all-gather.5.cloned.1.call-update) | async-done | bytes 16777232 | tf_op jit(solution)/shard_map/all_gather | solution.py:21
  213.5 1.6 broadcast_in_dim.54
  215.1 14.8 %select_convert_fusion = bf16[512,1024]{1,0:T(8,128)(2,1)S(1)} fusion(pred[64,8,8,128]{3,2,1,0:T(8,128)(4,1)S(1)} %bitcast.34, bf16[512,8192]{1,0:T(8,128)(2,1)} %all-gather.3.cloned.1.call-done, bf16[8192,1024]{1,0:T(8,128)(2,1)} %all-gather.5.cloned.1.call-done), kind=kOutput, calls=%fused_computation | convolution fusion | flops 8590983168 | bytes 26738688 | tf_op jit(solution)/shard_map/dot_general | solution.py:22
  229.9 0.1 dynamic-slice_bitcast_fusion.3
  230.0 0.1 pad_maximum_fusion
  230.2 0.3 collective-permute-start
  230.5 0.1 slice.30
  230.6 0.1 slice_reduce_fusion
  230.7 13.7 %collective-permute-done = bf16[2,256,1024]{2,1,0:T(8,128)(2,1)S(1)} collective-permute-done((bf16[2,256,1024]{2,1,0:T(8,128)(2,1)S(1)}, bf16[2,256,1024]{2,1,0:T(8,128)(2,1)S(1)}, u32[]{:S(2)}, u32[]{:S(2)}) %collective-permute-start) | collective-permute-done | bytes 1048608 | tf_op jit(solution)/shard_map/ppermute | solution.py:9
  244.5 0.2 broadcast_select_fusion
  244.6 4.7 %collective-permute-start.1 = (bf16[2,256,1024]{2,1,0:T(8,128)(2,1)S(1)}, bf16[2,256,1024]{2,1,0:T(8,128)(2,1)S(1)}, u32[]{:S(2)}, u32[]{:S(2)}) collective-permute-start(bf16[2,256,1024]{2,1,0:T(8,128)(2,1)S(1)} %broadcast_select_fusion), channel_id=1, source_target_pairs={{0,112},{8,120},{16,0},{24,8},{32,16},{40,24},{48,32},{56,40},{64,... | collective-permute-start | bytes 3145736 | tf_op jit(solution)/shard_map/ppermute | solution.py:9
  249.3 20.7 %collective-permute-done.1 = bf16[2,256,1024]{2,1,0:T(8,128)(2,1)S(1)} collective-permute-done((bf16[2,256,1024]{2,1,0:T(8,128)(2,1)S(1)}, bf16[2,256,1024]{2,1,0:T(8,128)(2,1)S(1)}, u32[]{:S(2)}, u32[]{:S(2)}) %collective-permute-start.1) | collective-permute-done | bytes 1048608 | tf_op jit(solution)/shard_map/ppermute | solution.py:9
  270.0 0.2 broadcast_select_fusion.1
  270.2 2.2 collective-permute-start.2
  272.4 22.7 %collective-permute-done.2 = bf16[2,256,1024]{2,1,0:T(8,128)(2,1)S(1)} collective-permute-done((bf16[2,256,1024]{2,1,0:T(8,128)(2,1)S(1)}, bf16[2,256,1024]{2,1,0:T(8,128)(2,1)S(1)}, u32[]{:S(2)}, u32[]{:S(2)}) %collective-permute-start.2) | collective-permute-done | bytes 1048608 | tf_op jit(solution)/shard_map/ppermute | solution.py:9
  295.1 0.2 broadcast_select_fusion.2
  295.3 2.1 collective-permute-start.3
  297.4 23.4 %collective-permute-done.3 = bf16[2,256,1024]{2,1,0:T(8,128)(2,1)S(1)} collective-permute-done((bf16[2,256,1024]{2,1,0:T(8,128)(2,1)S(1)}, bf16[2,256,1024]{2,1,0:T(8,128)(2,1)S(1)}, u32[]{:S(2)}, u32[]{:S(2)}) %collective-permute-start.3) | collective-permute-done | bytes 1048608 | tf_op jit(solution)/shard_map/ppermute | solution.py:9
  320.8 1.1 broadcast_select_fusion.3
  (10 shorter events, 0.1 us)
Async XLA Ops:
  6.5 9.8 %copy-start.1 = (s32[64]{0:T(128)S(1)}, s32[64]{0:T(128)}, u32[]{:S(2)}) copy-start(s32[64]{0:T(128)} %param.11) | copy-start | bytes 772
  6.5 13.1 %copy-start = (s32[4,8]{1,0:T(4,128)S(1)}, s32[4,8]{1,0:T(4,128)}, u32[]{:S(2)}) copy-start(s32[4,8]{1,0:T(4,128)} %param.10) | copy-start | bytes 388
  6.5 115.1 %all-gather.3.cloned.1.call-start = ((), (), s32[]{:S(2)}) async-start(), calls=%async_computation | async-start | bytes 9437184 | tf_op jit(solution)/shard_map/all_gather | solution.py:23
  11.4 202.1 %all-gather.5.cloned.1.call-start = ((), (), s32[]{:S(2)}) async-start(), calls=%async_computation.1 | async-start | bytes 17825792 | tf_op jit(solution)/shard_map/all_gather | solution.py:21
  230.2 14.3 %collective-permute-start = (bf16[2,256,1024]{2,1,0:T(8,128)(2,1)S(1)}, bf16[2,256,1024]{2,1,0:T(8,128)(2,1)S(1)}, u32[]{:S(2)}, u32[]{:S(2)}) collective-permute-start(bf16[2,256,1024]{2,1,0:T(8,128)(2,1)S(1)} %bitcast.30), channel_id=1, source_target_pairs={{0,120},{8,0},{16,8},{24,16},{32,24},{40,32},{48,40},{56,48},{64,5... | collective-permute-start | bytes 3145736 | tf_op jit(solution)/shard_map/ppermute | solution.py:9
  244.6 25.4 %collective-permute-start.1 = (bf16[2,256,1024]{2,1,0:T(8,128)(2,1)S(1)}, bf16[2,256,1024]{2,1,0:T(8,128)(2,1)S(1)}, u32[]{:S(2)}, u32[]{:S(2)}) collective-permute-start(bf16[2,256,1024]{2,1,0:T(8,128)(2,1)S(1)} %broadcast_select_fusion), channel_id=1, source_target_pairs={{0,112},{8,120},{16,0},{24,8},{32,16},{40,24},{48,32},{56,40},{64,... | collective-permute-start | bytes 3145736 | tf_op jit(solution)/shard_map/ppermute | solution.py:9
  270.2 24.9 %collective-permute-start.2 = (bf16[2,256,1024]{2,1,0:T(8,128)(2,1)S(1)}, bf16[2,256,1024]{2,1,0:T(8,128)(2,1)S(1)}, u32[]{:S(2)}, u32[]{:S(2)}) collective-permute-start(bf16[2,256,1024]{2,1,0:T(8,128)(2,1)S(1)} %broadcast_select_fusion.1), channel_id=1, source_target_pairs={{0,96},{8,104},{16,112},{24,120},{32,0},{40,8},{48,16},{56,24},{64... | collective-permute-start | bytes 3145736 | tf_op jit(solution)/shard_map/ppermute | solution.py:9
  295.3 25.5 %collective-permute-start.3 = (bf16[2,256,1024]{2,1,0:T(8,128)(2,1)S(1)}, bf16[2,256,1024]{2,1,0:T(8,128)(2,1)S(1)}, u32[]{:S(2)}, u32[]{:S(2)}) collective-permute-start(bf16[2,256,1024]{2,1,0:T(8,128)(2,1)S(1)} %broadcast_select_fusion.2), channel_id=1, source_target_pairs={{0,64},{8,72},{16,80},{24,88},{32,96},{40,104},{48,112},{56,120},{... | collective-permute-start | bytes 3145736 | tf_op jit(solution)/shard_map/ppermute | solution.py:9
Sparse Core Ops, SparseCore 0:
  11.5 110.0 all-gather.2
  123.3 90.1 all-gather.4
where the time goes:
time: 330 us; the launch traced here: 329 us
  waiting for transfers between devices  274 us (83%)
  between operations  16.1 us (5%)
  matrix products  14.8 us (4%)
  starting transfers between devices  9.3 us (3%)
  other arithmetic  8.29 us (3%)
  local copies, waits for them, and re-layouts  5.82 us (2%)
    all_gather x1, waiting for transfers between devices, local(): lax.all_gather(masked_a, 'col', axis=1, tiled=True)  102 us
    all_gather x1, waiting for transfers between devices, local(): b_panel = lax.all_gather(masked_b, 'row', axis=0, tiled=True)  91.9 us
    ppermute x4, waiting for transfers between devices, from_behind(): lax.ppermute(value, axis, [(i, (i + by) % count) for i in range(count)])  80.6 us
    dot_general x1, matrix products, local(): jnp.dot(lax.all_gather(masked_a, 'col', axis=1, tiled=True), b_panel, pre...  14.8 us
    ppermute x4, starting transfers between devices, from_behind(): lax.ppermute(value, axis, [(i, (i + by) % count) for i in range(count)])  9.25 us
  transfers between devices with their start and end apart: 6, of which 6 were waited for; matrix products, arithmetic and copies ran while one was open for 2% of the time, Pallas kernels for 0%

commit v1 on v0

--- a/solution.py
+++ b/solution.py
@@ -4,13 +4,17 @@
 from jax.sharding import PartitionSpec as P
 
 
-def from_behind(value, axis, by):
-    count = lax.axis_size(axis)
-    return lax.ppermute(value, axis, [(i, (i + by) % count) for i in range(count)])
+def expand(pattern, width):
+    return jnp.repeat(jnp.repeat(pattern, width, axis=0), width, axis=1)
 
 
-def expand(pattern, width):
-    return jnp.repeat(jnp.repeat(pattern, width, axis=0), width, axis=1)
+def shifted(value, axis, shift):
+    count = lax.axis_size(axis)
+
+    def branch(by):
+        return lambda v: lax.ppermute(v, axis, [((i + by) % count, i) for i in range(count)])
+
+    return lax.switch(shift - 1, [branch(by) for by in range(1, count)], value)
 
 
 def local(a_values, b_values, a_pattern, b_pattern, c_pattern, owner_list):
@@ -30,17 +34,11 @@
     blocks_here = a_pattern.shape[0]
     slot_shift = owner_list[:blocks_here] // blocks_here % row_count
     slot_source = owner_list[:blocks_here] % blocks_here
-    pieces = []
-    for slot in range(blocks_here):
-        pieces.append(lax.dynamic_slice_in_dim(rounded, slot_source[slot] * width, width, 0))
-    moving = jnp.stack(pieces, axis=0).reshape(blocks_here // 2, 2 * width, local_cols)
-    pair_shift = slot_shift.reshape(blocks_here // 2, 2)[:, 0]
-    steps_needed = (row_count - 1).bit_length()
-    for level in range(steps_needed):
-        arrived = from_behind(moving, "row", row_count - (1 << level))
-        taken = pair_shift // (1 << level) % 2 > 0
-        moving = jnp.where(taken[:, None, None], arrived, moving)
-    return moving.reshape(blocks_here * width, local_cols)
+    out = []
+    for pair in range(blocks_here // 2):
+        rows = [lax.dynamic_slice_in_dim(rounded, slot_source[2 * pair + t] * width, width, 0) for t in range(2)]
+        out.append(shifted(jnp.concatenate(rows, axis=0), "row", slot_shift[2 * pair]))
+    return jnp.concatenate(out, axis=0)
 
 
 def solution(mesh):

time: 330 us -> 269 us (0.82)
  waiting for transfers between devices: 274 us -> 212 us
    ppermute x4 -> x2, waiting for transfers between devices: 80.6 us -> 20 us  [branch(): lax.ppermute(v, axis, [((i + by) % count, i) for i in range(count)])]
    ppermute x4 -> x2, starting transfers between devices: 9.25 us -> 7.96 us  [branch(): lax.ppermute(v, axis, [((i + by) % count, i) for i in range(count)])]
  transfers between devices with their start and end apart: 6 -> 4, of which waited for: 6 -> 4; matrix products, arithmetic and copies ran while one was open for 2% -> 2% of each run, Pallas kernels for 0% -> 0%
where the time goes in v1:
time: 269 us; the launch traced here: 267 us
  waiting for transfers between devices  212 us (79%)
  between operations  17.5 us (7%)
  matrix products  14.8 us (6%)
  other arithmetic  8.7 us (3%)
  starting transfers between devices  8.01 us (3%)
  local copies, waits for them, and re-layouts  6.31 us (2%)
    all_gather x1, waiting for transfers between devices, local(): lax.all_gather(masked_a, 'col', axis=1, tiled=True)  100 us
    all_gather x1, waiting for transfers between devices, local(): b_panel = lax.all_gather(masked_b, 'row', axis=0, tiled=True)  91.9 us
    ppermute x2, waiting for transfers between devices, branch(): lax.ppermute(v, axis, [((i + by) % count, i) for i in range(count)])  20 us
    dot_general x1, matrix products, local(): jnp.dot(lax.all_gather(masked_a, 'col', axis=1, tiled=True), b_panel, pre...  14.8 us
    ppermute x2, starting transfers between devices, branch(): lax.ppermute(v, axis, [((i + by) % count, i) for i in range(count)])  7.96 us
  transfers between devices with their start and end apart: 4, of which 4 were waited for; matrix products, arithmetic and copies ran while one was open for 2% of the time, Pallas kernels for 0%

profile of v1, /device:TPU:1, one launch (start us, length us, event | category | flops | bytes accessed | tf_op | source)
XLA Modules:
  0.0 267.2 jit_solution(13233717530644523407)
XLA Ops:
  6.5 0.0 copy-start.1
  6.5 0.0 copy-start
  6.5 0.0 all-gather.3.cloned.1.call-start
  6.5 0.7 broadcast_compare_fusion.1
  7.3 1.6 broadcast_in_dim.25
  8.9 2.5 bitcast_select_fusion.1
  11.4 0.0 all-gather.3.cloned.1.call-update
  11.4 0.0 all-gather.5.cloned.1.call-start
  11.4 0.7 broadcast_compare_fusion
  12.2 1.6 broadcast_in_dim.27
  13.8 2.5 bitcast_select_fusion
  16.3 0.0 all-gather.5.cloned.1.call-update
  16.3 0.0 copy-done.1
  16.3 0.7 fusion.1
  19.6 0.7 fusion.2
  21.6 0.0 copy-done
  21.6 100.0 %all-gather.3.cloned.1.call-done = bf16[512,8192]{1,0:T(8,128)(2,1)} async-done(((bf16[512,1024]{1,0:T(8,128)(2,1)}), bf16[512,8192]{1,0:T(8,128)(2,1)}) %all-gather.3.cloned.1.call-update) | async-done | bytes 8388624 | tf_op jit(solution)/shard_map/all_gather | solution.py:27
  121.6 91.9 %all-gather.5.cloned.1.call-done = bf16[8192,1024]{1,0:T(8,128)(2,1)} async-done(((bf16[512,1024]{1,0:T(8,128)(2,1)}), bf16[8192,1024]{1,0:T(8,128)(2,1)}) %all-gather.5.cloned.1.call-update) | async-done | bytes 16777232 | tf_op jit(solution)/shard_map/all_gather | solution.py:25
  213.5 1.6 broadcast_in_dim.23
  215.1 14.8 %select_convert_fusion = bf16[512,1024]{1,0:T(8,128)(2,1)S(1)} fusion(pred[64,8,8,128]{3,2,1,0:T(8,128)(4,1)S(1)} %bitcast.22, bf16[512,8192]{1,0:T(8,128)(2,1)} %all-gather.3.cloned.1.call-done, bf16[8192,1024]{1,0:T(8,128)(2,1)} %all-gather.5.cloned.1.call-done), kind=kOutput, calls=%fused_computation | convolution fusion | flops 8590983168 | bytes 26738688 | tf_op jit(solution)/shard_map/dot_general | solution.py:26
  230.0 0.1 constant_dynamic-slice_fusion.3
  230.0 0.1 pad_maximum_fusion.1
  230.1 13.7 %conditional.3 = (bf16[256,1024]{1,0:T(8,128)(2,1)}) conditional(s32[]{:T(128)} %bitcast.6, bf16[256,1024]{1,0:T(8,128)(2,1)S(1)} %get-tuple-element.80, bf16[256,1024]{1,0:T(8,128)(2,1)S(1)} %get-tuple-element.80, bf16[256,1024]{1,0:T(8,128)(2,1)S(1)} %get-tuple-element.80, ...), branch_computations={%region_15.16_spmd, %region_16.17_spmd, %region_17.18_spmd, %regio... | conditional | bytes 2097200 | solution.py:17
  230.1 2.6 collective-permute-start.16
  232.7 11.1 %collective-permute-done.16 = bf16[256,1024]{1,0:T(8,128)(2,1)} collective-permute-done((bf16[256,1024]{1,0:T(8,128)(2,1)S(1)}, bf16[256,1024]{1,0:T(8,128)(2,1)}, u32[]{:S(2)}, u32[]{:S(2)}) %collective-permute-start.16) | collective-permute-done | bytes 524320 | tf_op jit(solution)/shard_map/cond/branch_1_fun/ppermute | solution.py:15
  243.8 14.3 %conditional.2 = (bf16[256,1024]{1,0:T(8,128)(2,1)}) conditional(s32[]{:T(128)} %bitcast, bf16[256,1024]{1,0:T(8,128)(2,1)S(1)} %get-tuple-element.79, bf16[256,1024]{1,0:T(8,128)(2,1)S(1)} %get-tuple-element.79, bf16[256,1024]{1,0:T(8,128)(2,1)S(1)} %get-tuple-element.79, ...), branch_computations={%region_0.1_spmd, %region_1.2_spmd, %region_2.3_spmd, %region_3.4_... | conditional | bytes 2097200 | solution.py:17
  243.8 5.4 %collective-permute-start.2 = (bf16[256,1024]{1,0:T(8,128)(2,1)S(1)}, bf16[256,1024]{1,0:T(8,128)(2,1)}, u32[]{:S(2)}, u32[]{:S(2)}) collective-permute-start(bf16[256,1024]{1,0:T(8,128)(2,1)S(1)} %param.2), channel_id=1, source_target_pairs={{24,0},{32,8},{40,16},{48,24},{56,32},{64,40},{72,48},{80,56},{88,... | collective-permute-start | bytes 1572872 | tf_op jit(solution)/shard_map/cond/branch_2_fun/ppermute | solution.py:15
  249.2 9.0 %collective-permute-done.2 = bf16[256,1024]{1,0:T(8,128)(2,1)} collective-permute-done((bf16[256,1024]{1,0:T(8,128)(2,1)S(1)}, bf16[256,1024]{1,0:T(8,128)(2,1)}, u32[]{:S(2)}, u32[]{:S(2)}) %collective-permute-start.2) | collective-permute-done | bytes 524320 | tf_op jit(solution)/shard_map/cond/branch_2_fun/ppermute | solution.py:15
  258.1 2.2 pad_maximum_fusion
  (6 shorter events, 0.1 us)
Async XLA Ops:
  6.5 9.7 %copy-start.1 = (s32[64]{0:T(128)S(1)}, s32[64]{0:T(128)}, u32[]{:S(2)}) copy-start(s32[64]{0:T(128)} %param.41) | copy-start | bytes 772
  6.5 15.1 %copy-start = (s32[4,8]{1,0:T(4,128)S(1)}, s32[4,8]{1,0:T(4,128)}, u32[]{:S(2)}) copy-start(s32[4,8]{1,0:T(4,128)} %param.40) | copy-start | bytes 388
  6.5 115.1 %all-gather.3.cloned.1.call-start = ((), (), s32[]{:S(2)}) async-start(), calls=%async_computation | async-start | bytes 9437184 | tf_op jit(solution)/shard_map/all_gather | solution.py:27
  11.4 202.1 %all-gather.5.cloned.1.call-start = ((), (), s32[]{:S(2)}) async-start(), calls=%async_computation.1 | async-start | bytes 17825792 | tf_op jit(solution)/shard_map/all_gather | solution.py:25
  230.1 13.7 %collective-permute-start.16 = (bf16[256,1024]{1,0:T(8,128)(2,1)S(1)}, bf16[256,1024]{1,0:T(8,128)(2,1)}, u32[]{:S(2)}, u32[]{:S(2)}) collective-permute-start(bf16[256,1024]{1,0:T(8,128)(2,1)S(1)} %param.16), channel_id=1, source_target_pairs={{16,0},{24,8},{32,16},{40,24},{48,32},{56,40},{64,48},{72,56},{80,... | collective-permute-start | bytes 1572872 | tf_op jit(solution)/shard_map/cond/branch_1_fun/ppermute | solution.py:15
  243.8 14.3 %collective-permute-start.2 = (bf16[256,1024]{1,0:T(8,128)(2,1)S(1)}, bf16[256,1024]{1,0:T(8,128)(2,1)}, u32[]{:S(2)}, u32[]{:S(2)}) collective-permute-start(bf16[256,1024]{1,0:T(8,128)(2,1)S(1)} %param.2), channel_id=1, source_target_pairs={{24,0},{32,8},{40,16},{48,24},{56,32},{64,40},{72,48},{80,56},{88,... | collective-permute-start | bytes 1572872 | tf_op jit(solution)/shard_map/cond/branch_2_fun/ppermute | solution.py:15
Sparse Core Ops, SparseCore 0:
  11.5 110.0 all-gather.2
  123.3 90.1 all-gather.4
